TPU v7x, 32 devices: a whole 2x2x4 slice. The times are simulated.
32 devices in a mesh: lat: 8 (over z, x), lev: 4 (over y, core).
Axes of the slice: x: 2, y: 2, z: 4, core: 2. Of those that a mesh axis runs over, the one named last changes fastest.
Arguments:
- particle_mass_fraction: float32 [20, 64, 8, 360], P(None, 'lat', 'lev'), may hold values from 0.1 to 2
- meridional_cfl_factor: float32 [64, 8, 360], P('lat', 'lev'), may hold values from -0.45 to 0.45
- thermal_state_kelvins: float32 [64, 8, 360], P('lat', 'lev'), may hold values from 200 to 300
- logarithmic_barometric_span: float32 [8], P('lev'), may hold values from 0.06 to 0.2
- gravitational_fall_kilometres: float32 [20], replicated, may hold values from 0.02 to 20
- zonal_cfl_factor: float32 [64, 8, 360], P('lat', None, 'lev'), may hold values from -0.45 to 0.45
- collision_rate_matrix: float32 [20, 20], replicated, may hold values from 0.02 to 0.2
Outputs:
- dust_out: float32 [20, 64, 8, 360], P(None, 'lat', None, 'lev')
- height: float32 [64, 8, 360], P('lat', 'lev')
All inputs are finite; a program needn't handle non-finite values.
Results may differ from a plain program's by a relative error of at most 0.000067.
Values sent between devices are 32-bit elements; how exact they have to be, the bound alone decides.
A program may use at most 128 MiB of HBM per device.

v0:
```python
import jax
import jax.numpy as jnp
from jax import lax
from jax.sharding import PartitionSpec as P

specific_air_factor = 0.0293
scale_height = 7.0


def extended_2(x, sides, width, wrap):
    for axis, dim in sides:
        peers, length = (lax.axis_size(axis), x.shape[dim])
        up = [(i, (i + 1) % peers) for i in range(peers if wrap else peers - 1)]
        down = [(j, i) for i, j in up]
        last = lax.slice_in_dim(x, length - width, length, axis=dim)
        leading = lax.slice_in_dim(x, 0, width, axis=dim)
        before = lax.ppermute(last, axis, up)
        after = lax.ppermute(leading, axis, down)
        x = jnp.concatenate([before, x, after], axis=dim)
    return x


def prefix(value, axis, join, neutral):
    count, mine = (lax.axis_size(axis), lax.axis_index(axis))
    pieces = lax.all_gather(value, axis)
    pieces = pieces[::-1]
    mine = count - 1 - mine
    subtotal = jnp.full_like(value, 0) + jnp.asarray(neutral, value.dtype)

    def step(position, subtotal):
        longer = join(subtotal, pieces[position])
        return jnp.where(position < mine, longer, subtotal)

    return lax.fori_loop(0, count - 1, step, subtotal)


def settle_sweep(mixing, settle_rate, inflow):

    def stepper(flux_in, inputs):
        level_mix, level_rate = inputs
        summed = level_mix + flux_in
        return (level_rate / (1.0 + level_rate) * summed, summed / (1.0 + level_rate))

    _, swept = lax.scan(
        stepper, inflow, (jnp.moveaxis(mixing, 2, 0), jnp.moveaxis(settle_rate, 2, 0))
    )
    return jnp.moveaxis(swept, 0, 2)


def add_terms(earlier, later):
    return earlier + later


def on_device(
    particle_mass_fraction,
    meridional_cfl_factor,
    thermal_state_kelvins,
    logarithmic_barometric_span,
    gravitational_fall_kilometres,
    zonal_cfl_factor,
    collision_rate_matrix,
):
    bin_count = particle_mass_fraction.shape[0]
    stacked = jnp.concatenate([particle_mass_fraction, meridional_cfl_factor[None]], 0)
    padded = extended_2(stacked, (("lat", 1),), 1, False)
    rows_below = padded[:bin_count, :-2]
    rows_above = padded[:bin_count, 2:]
    courant_above = padded[bin_count, 2:]
    south_flux = (
        jnp.maximum(meridional_cfl_factor, 0.0) * rows_below
        + jnp.minimum(meridional_cfl_factor, 0.0) * particle_mass_fraction
    )
    north_flux = (
        jnp.maximum(courant_above, 0.0) * particle_mass_fraction
        + jnp.minimum(courant_above, 0.0) * rows_above
    )
    advected = particle_mass_fraction + south_flux - north_flux
    vertical_span_height = (
        specific_air_factor * thermal_state_kelvins * logarithmic_barometric_span[None, :, None]
    )
    column_total = jnp.sum(vertical_span_height, axis=1)
    incoming = prefix(column_total, "lev", add_terms, jnp.zeros_like(column_total))
    height = (
        incoming[:, None, :]
        + jnp.cumsum(vertical_span_height[:, ::-1], axis=1)[:, ::-1]
        - 0.5 * vertical_span_height
    )
    density = jnp.exp(-height / scale_height)
    packed = jnp.concatenate([advected, vertical_span_height[None], density[None]], 0)
    columns = lax.all_to_all(packed, "lev", split_axis=3, concat_axis=2, tiled=True)
    col_thick = columns[bin_count]
    col_density = columns[bin_count + 1]
    settle_rate = gravitational_fall_kilometres[:, None, None, None] / col_thick[None]
    inflow = jnp.zeros((bin_count, columns.shape[1], columns.shape[3]), jnp.float32)
    settled = settle_sweep(columns[:bin_count], settle_rate, inflow)
    extended = extended_2(
        jnp.concatenate([settled, zonal_cfl_factor[None]], 0), (("lev", 3),), 1, True
    )
    west_mix = extended[:bin_count, :, :, :-2]
    east_mix = extended[:bin_count, :, :, 2:]
    courant_east = extended[bin_count, :, :, 2:]
    west_flux = (
        jnp.maximum(zonal_cfl_factor, 0.0) * west_mix + jnp.minimum(zonal_cfl_factor, 0.0) * settled
    )
    east_flux = jnp.maximum(courant_east, 0.0) * settled + jnp.minimum(courant_east, 0.0) * east_mix
    moved = settled + west_flux - east_flux
    merging = jnp.tril(collision_rate_matrix, -1) - jnp.triu(collision_rate_matrix, 1)
    coag_rate = jnp.einsum("bc,clkx->blkx", merging, moved, precision=lax.Precision.HIGHEST)
    return (moved + col_density * moved * coag_rate, height)


def solution(mesh):
    in_specs = (
        P(None, "lat", "lev", None),
        P("lat", "lev", None),
        P("lat", "lev", None),
        P("lev"),
        P(),
        P("lat", None, "lev"),
        P(),
    )
    out_specs = (P(None, "lat", None, "lev"), P("lat", "lev", None))
    return jax.shard_map(
        on_device, mesh=mesh, in_specs=in_specs, out_specs=out_specs, check_vma=False
    )
```

profile of v0, /device:TPU:0, one launch (start us, length us, event | category | flops | bytes accessed | tf_op | source)
XLA Modules:
  0.0 57.4 jit_solution(17528665692314259171)
XLA Ops:
  0.6 1.0 %pad_maximum_fusion.11 = (f32[21,1,2,360]{3,2,1,0:T(2,128)S(1)}, f32[21,1,2,360]{3,2,1,0:T(2,128)S(1)}) fusion(f32[1,8,2,360]{3,2,1,0:T(2,128)} %bitcast.67, f32[20,8,2,360]{3,2,1,0:T(2,128)} %param.11), kind=kLoop, calls=%fused_computation.41 | loop fusion | flops 30240 | bytes 604800 | tf_op jit(solution)/shard_map/slice | solution.py:15
  1.7 1.3 %collective-permute-start.1 = (f32[21,1,2,360]{3,2,1,0:T(2,128)S(1)}, f32[21,1,2,360]{3,2,1,0:T(2,128)S(1)}, u32[]{:S(2)}, u32[]{:S(2)}) collective-permute-start(f32[21,1,2,360]{3,2,1,0:T(2,128)S(1)} %get-tuple-element.233), channel_id=1, source_target_pairs={{4,0},{8,4},{12,8},{16,12},{20,16},{24,20},{28,24},{5,1},{9,5},{13... | collective-permute-start | bytes 181448 | tf_op jit(solution)/shard_map/ppermute | solution.py:18
  3.0 5.5 %collective-permute-start = (f32[21,1,2,360]{3,2,1,0:T(2,128)S(1)}, f32[21,1,2,360]{3,2,1,0:T(2,128)S(1)}, u32[]{:S(2)}, u32[]{:S(2)}) collective-permute-start(f32[21,1,2,360]{3,2,1,0:T(2,128)S(1)} %get-tuple-element.232), channel_id=1, source_target_pairs={{0,4},{4,8},{8,12},{12,16},{16,20},{20,24},{24,28},{1,5},{5,9},{9,... | collective-permute-start | bytes 181448 | tf_op jit(solution)/shard_map/ppermute | solution.py:17
  8.4 0.8 %broadcast_maximum_fusion.2 = (f32[8,2,360]{2,1,0:T(2,128)S(1)}, f32[8,2,360]{2,1,0:T(2,128)S(1)}) fusion(f32[8,2,360]{2,1,0:T(2,128)} %param.12), kind=kLoop, calls=%fused_computation.60 | loop fusion | flops 11520 | bytes 69120 | tf_op jit(solution)/shard_map/max | solution.py:70
  9.2 0.7 %broadcast_multiply_fusion = f32[2]{0:T(128)S(1)} fusion(f32[2]{0:T(128)} %param.14), kind=kLoop, calls=%fused_computation.64 | loop fusion | flops 2 | bytes 16 | tf_op jit(solution)/shard_map/mul | solution.py:79
  9.9 0.8 %fusion.29 = (f32[8,360]{1,0:T(8,128)S(1)}, f32[8,2,360]{2,0,1:T(8,128)S(1)}) fusion(f32[2]{0:T(128)S(1)} %broadcast_multiply_fusion, f32[8,2,360]{2,1,0:T(2,128)} %param.13), kind=kLoop, calls=%fused_computation.67 | loop fusion | flops 8640 | bytes 57608 | tf_op jit(solution)/shard_map/reduce_sum | solution.py:81
  10.8 5.3 %all-gather = f32[32,360]{1,0:T(8,128)S(1)} all-gather(f32[8,360]{1,0:T(8,128)S(1)} %get-tuple-element.224), channel_id=2, replica_groups=mesh['lat'=8,'lev'=4] {'lev'}, dimensions={0}, use_global_device_ids=true | all-gather | bytes 57600 | tf_op jit(solution)/shard_map/all_gather | solution.py:25
  16.2 0.6 %exponential_bitcast_fusion = (f32[1,8,2,360]{3,1,2,0:T(8,128)S(1)}, f32[8,2,360]{2,0,1:T(8,128)}) fusion(f32[8,2,360]{2,0,1:T(8,128)S(1)} %get-tuple-element.225, f32[8,2,360]{2,0,1:T(8,128)S(1)} %fusion.31, f32[8,360]{1,0:T(8,128)S(1)} %get-tuple-element.108), kind=kLoop, calls=%fused_computation.45 | loop fusion | flops 28800 | bytes 103680 | tf_op jit(solution)/shard_map/broadcast_in_dim | solution.py:89
  16.8 0.8 %maximum_bitcast_fusion = (f32[8,2,360]{2,1,0:T(2,128)S(1)}, f32[1,8,2,360]{3,2,1,0:T(2,128)S(1)}) fusion(f32[21,1,2,360]{3,2,1,0:T(2,128)S(1)} %collective-permute-done.1, f32[1,8,2,360]{3,2,1,0:T(2,128)} %bitcast.68, f32[20,8,2,360]{3,2,1,0:T(2,128)} %param.11), kind=kLoop, calls=%fused_computation.48 | loop fusion | flops 17280 | bytes 590400 | tf_op jit(solution)/shard_map/mul | solution.py:74
  17.7 1.7 %pad_maximum_fusion.8 = (f32[20,8,2,360]{3,2,1,0:T(2,128)S(1)}, f32[20,8,2,360]{3,2,1,0:T(2,128)S(1)}) fusion(f32[21,1,2,360]{3,2,1,0:T(2,128)S(1)} %collective-permute-done, f32[1,8,2,360]{3,2,1,0:T(2,128)} %bitcast.69, f32[20,8,2,360]{3,2,1,0:T(2,128)} %param.11, f32[21,1,2,360]{3,2,1,0:T(2,128)S(1)} %collective-permute-done.1), kind=kLoop, calls=%fused_computation.27 | loop fusion | flops 460800 | bytes 1526400 | tf_op jit(solution)/shard_map/concatenate | solution.py:19
  19.6 1.3 %copy.255 = f32[22,8,2,360]{0,1,2,3:T(8,128)S(1)} copy(f32[22,8,2,360]{3,1,2,0:T(8,128)S(1)} %pad_maximum_fusion.5) | data formatting | bytes 1013760 | tf_op jit(solution)/shard_map/concatenate | solution.py:89
  20.9 3.7 %reshape.18 = f32[4,1,31680]{2,1,0:T(1,128)} reshape(f32[360,2,8,22]{3,2,1,0:T(8,128)S(1)} %bitcast.60) | data formatting | bytes 1013760
  24.6 3.5 %all-to-all-start = ((f32[4,1,31680]{2,1,0:T(1,128)}), f32[4,1,31680]{2,1,0:T(1,128)S(1)}, u32[]{:S(2)}, u32[]{:S(2)}) async-start(f32[4,1,31680]{2,1,0:T(1,128)} %reshape.18), calls=%async_computation | async-start | bytes 1015808 | tf_op jit(solution)/shard_map/all_to_all | solution.py:90
  28.1 0.6 %broadcast_maximum_fusion.1 = (f32[8,8,90]{2,1,0:T(8,128)}, f32[8,8,90]{2,1,0:T(8,128)}) fusion(f32[8,8,90]{2,1,0:T(8,128)S(1)} %copy-done.2), kind=kLoop, calls=%fused_computation.52 | loop fusion | flops 11520 | bytes 69120 | tf_op jit(solution)/shard_map/max | solution.py:103
  28.7 8.1 %all-to-all-done = f32[4,1,31680]{2,1,0:T(1,128)S(1)} async-done(((f32[4,1,31680]{2,1,0:T(1,128)}), f32[4,1,31680]{2,1,0:T(1,128)S(1)}, u32[]{:S(2)}, u32[]{:S(2)}) %all-to-all-start) | async-done | bytes 506912 | tf_op jit(solution)/shard_map/all_to_all | solution.py:90
  36.8 0.6 %broadcast.65 = f32[]{:T(128)} broadcast(f32[]{:T(128)} %constant.131), dimensions={} | broadcast | bytes 8 | tf_op jit(solution)/shard_map/all_to_all | solution.py:90
  37.4 2.2 %reduce = f32[4,31680]{1,0:T(4,128)S(1)} reduce(f32[4,1,31680]{2,1,0:T(1,128)S(1)} %all-to-all-done, f32[]{:T(128)} %broadcast.65), dimensions={1}, to_apply=%all_to_all.11.reduce_sub_computation | reduce | bytes 1013764 | tf_op jit(solution)/shard_map/all_to_all | solution.py:90
  39.6 3.5 %reshape.19 = f32[360,2,8,22]{3,2,1,0:T(8,128)S(1)} reshape(f32[4,31680]{1,0:T(4,128)S(1)} %reduce) | data formatting | bytes 1013760
  43.1 2.2 %copy.270 = f32[22,8,2,4,90]{4,3,1,2,0:T(4,128)} copy(f32[22,8,2,4,90]{0,1,2,4,3:T(8,128)S(1)} %bitcast.59) | data formatting | bytes 1013760 | tf_op jit(solution)/shard_map/all_to_all | solution.py:90
  45.3 0.8 %fusion.30 = (f32[1,8,4,2,90]{4,2,1,3,0:T(4,128)S(1)}, f32[1,8,4,2,90]{4,2,1,3,0:T(4,128)S(1)}) fusion(f32[22,8,4,2,90]{4,2,1,3,0:T(4,128)} %bitcast.65), kind=kLoop, calls=%fused_computation.68 | loop fusion | bytes 92160 | tf_op jit(solution)/shard_map/slice | solution.py:92
  46.1 1.1 %slice.65 = f32[20,8,4,2,90]{4,2,1,3,0:T(4,128)S(1)} slice(f32[22,8,4,2,90]{4,2,1,3,0:T(4,128)} %bitcast.66), slice={[0:20], [0:8], [0:4], [0:2], [0:90]} | slice | bytes 921600 | tf_op jit(solution)/shard_map/slice | solution.py:95
  47.5 0.8 %while.28 = (s32[]{:T(128)}, f32[20,8,90]{2,1,0:T(8,128)S(1)}, f32[8,20,8,90]{3,2,1,0:T(8,128)S(1)}, f32[8,20,8,90]{3,2,1,0:T(8,128)S(1)}, f32[8,20,8,90]{3,2,1,0:T(8,128)S(1)}, /*index=5*/s32[]{:T(128)}, s32[]{:T(128)}) while((s32[]{:T(128)}, f32[20,8,90]{2,1,0:T(8,128)S(1)}, f32[8,20,8,90]{3,2,1,0:T(8,128)S(1)}, ...), condition=%wide.region_5.6_spmd.clone, body=%wide.region_4.5_spmd.clone.sunk | while | flops 129603 | bytes 558176 | solution.py:44
  48.5 0.4 slice_maximum_fusion
  48.9 0.5 copy.263
  49.4 0.6 %copy.268 = f32[8,2,360]{2,1,0:T(2,128)} copy(f32[8,2,360]{2,0,1:T(8,128)S(1)} %copy-done.4) | data formatting | bytes 46080
  50.0 0.5 copy.261
  50.5 0.7 %collective-permute-start.2 = (f32[21,8,8,1]{0,2,3,1:T(8,128)S(1)}, f32[21,8,8,1]{0,2,3,1:T(8,128)S(1)}, u32[]{:S(2)}, u32[]{:S(2)}) collective-permute-start(f32[21,8,8,1]{0,2,3,1:T(8,128)S(1)} %copy.261), channel_id=1, source_target_pairs={{0,1},{1,2},{2,3},{3,0},{4,5},{5,6},{6,7},{7,4},{8,9},{9,10},{10,1... | collective-permute-start | bytes 16136 | tf_op jit(solution)/shard_map/ppermute | solution.py:17
  51.2 0.5 copy.264
  52.0 2.0 %collective-permute-done.2 = f32[21,8,8,1]{0,2,3,1:T(8,128)S(1)} collective-permute-done((f32[21,8,8,1]{0,2,3,1:T(8,128)S(1)}, f32[21,8,8,1]{0,2,3,1:T(8,128)S(1)}, u32[]{:S(2)}, u32[]{:S(2)}) %collective-permute-start.2) | collective-permute-done | bytes 5408 | tf_op jit(solution)/shard_map/ppermute | solution.py:17
  54.1 0.5 copy.262
  54.6 1.9 %fusion.3 = f32[20,8,8,90]{3,0,2,1:T(8,128)S(1)} fusion(f32[21,8,8,1]{3,0,2,1:T(8,128)S(1)} %copy.264, f32[1,8,8,90]{3,0,2,1:T(1,128)S(1)} %bitcast.73, f32[20,8,8,90]{3,0,2,1:T(8,128)S(1)} %bitcast.63, f32[21,8,8,1]{3,0,2,1:T(8,128)S(1)} %copy.262, f32[8,8,90]{2,1,0:T(8,128)S(1)} %copy.266, f32[8,8,90]{2,1,0:T(8,128)S(1)} %bitcast.78, ...), kind=kOutput, calls=%fused_computation.8 | convolution fusion | flops 30760400 | bytes 1072272 | tf_op jit(solution)/shard_map/bc,clkx->blkx/dot_general | solution.py:108
  56.5 1.0 %copy.267 = f32[20,8,8,90]{3,2,1,0:T(8,128)} copy(f32[20,8,8,90]{3,0,2,1:T(8,128)S(1)} %fusion.3) | data formatting | bytes 921600
  (64 shorter events, 1.7 us)
Async XLA Ops:
  0.6 18.8 %copy-start = (f32[20,8,2,360]{3,2,1,0:T(2,128)S(1)}, f32[20,8,2,360]{3,2,1,0:T(2,128)}, u32[]{:S(2)}) copy-start(f32[20,8,2,360]{3,2,1,0:T(2,128)} %param.11) | copy-start | bytes 1382404
  1.7 15.2 %collective-permute-start.1 = (f32[21,1,2,360]{3,2,1,0:T(2,128)S(1)}, f32[21,1,2,360]{3,2,1,0:T(2,128)S(1)}, u32[]{:S(2)}, u32[]{:S(2)}) collective-permute-start(f32[21,1,2,360]{3,2,1,0:T(2,128)S(1)} %get-tuple-element.233), channel_id=1, source_target_pairs={{4,0},{8,4},{12,8},{16,12},{20,16},{24,20},{28,24},{5,1},{9,5},{13... | collective-permute-start | bytes 181448 | tf_op jit(solution)/shard_map/ppermute | solution.py:18
  3.0 14.7 %collective-permute-start = (f32[21,1,2,360]{3,2,1,0:T(2,128)S(1)}, f32[21,1,2,360]{3,2,1,0:T(2,128)S(1)}, u32[]{:S(2)}, u32[]{:S(2)}) collective-permute-start(f32[21,1,2,360]{3,2,1,0:T(2,128)S(1)} %get-tuple-element.232), channel_id=1, source_target_pairs={{0,4},{4,8},{8,12},{12,16},{16,20},{20,24},{24,28},{1,5},{5,9},{9,... | collective-permute-start | bytes 181448 | tf_op jit(solution)/shard_map/ppermute | solution.py:17
  20.9 7.2 %copy-start.2 = (f32[8,8,90]{2,1,0:T(8,128)S(1)}, f32[8,8,90]{2,1,0:T(8,128)}, u32[]{:S(2)}) copy-start(f32[8,8,90]{2,1,0:T(8,128)} %param.16) | copy-start | bytes 69124
  24.6 12.3 %all-to-all-start = ((f32[4,1,31680]{2,1,0:T(1,128)}), f32[4,1,31680]{2,1,0:T(1,128)S(1)}, u32[]{:S(2)}, u32[]{:S(2)}) async-start(f32[4,1,31680]{2,1,0:T(1,128)} %reshape.18), calls=%async_computation | async-start | bytes 1015808 | tf_op jit(solution)/shard_map/all_to_all | solution.py:90
  43.1 4.3 %copy-start.7 = (f32[20]{0:T(128)S(1)}, f32[20]{0:T(128)}, u32[]{:S(2)}) copy-start(f32[20]{0:T(128)} %param.15) | copy-start | bytes 244
  45.3 2.2 %copy-start.1 = (f32[8,20,8,90]{3,2,1,0:T(8,128)S(1)}, f32[8,20,8,90]{3,2,1,0:T(8,128)}, u32[]{:S(2)}) copy-start(f32[8,20,8,90]{3,2,1,0:T(8,128)} %custom-call.2) | copy-start | bytes 1382404
  47.3 1.1 %copy-start.3 = (f32[8,8,90]{2,1,0:T(8,128)S(1)}, f32[8,8,90]{2,1,0:T(8,128)}, u32[]{:S(2)}) copy-start(f32[8,8,90]{2,1,0:T(8,128)} %param.16) | copy-start | bytes 69124
  48.3 1.1 %copy-start.4 = (f32[8,2,360]{2,0,1:T(8,128)S(1)}, f32[8,2,360]{2,0,1:T(8,128)}, u32[]{:S(2)}) copy-start(f32[8,2,360]{2,0,1:T(8,128)} %get-tuple-element.223) | copy-start | bytes 69124
  48.8 5.7 %copy-start.5 = (f32[8,8,90]{2,1,0:T(8,128)S(1)}, f32[8,8,90]{2,1,0:T(8,128)}, u32[]{:S(2)}) copy-start(f32[8,8,90]{2,1,0:T(8,128)} %get-tuple-element.234) | copy-start | bytes 69124
  48.8 5.7 %copy-start.6 = (f32[8,8,90]{2,1,0:T(8,128)S(1)}, f32[8,8,90]{2,1,0:T(8,128)}, u32[]{:S(2)}) copy-start(f32[8,8,90]{2,1,0:T(8,128)} %get-tuple-element.235) | copy-start | bytes 69124
  48.9 5.7 %copy-start.8 = (f32[20,20]{1,0:T(8,128)S(1)}, f32[20,20]{1,0:T(8,128)}, u32[]{:S(2)}) copy-start(f32[20,20]{1,0:T(8,128)} %param.17) | copy-start | bytes 4804
  49.3 1.9 %collective-permute-start.3 = (f32[21,8,8,1]{0,2,3,1:T(8,128)S(1)}, f32[21,8,8,1]{0,2,3,1:T(8,128)S(1)}, u32[]{:S(2)}, u32[]{:S(2)}) collective-permute-start(f32[21,8,8,1]{0,2,3,1:T(8,128)S(1)} %copy.263), channel_id=1, source_target_pairs={{1,0},{2,1},{3,2},{0,3},{5,4},{6,5},{7,6},{4,7},{9,8},{10,9},{11,1... | collective-permute-start | bytes 16136 | tf_op jit(solution)/shard_map/ppermute | solution.py:18
  50.5 3.5 %collective-permute-start.2 = (f32[21,8,8,1]{0,2,3,1:T(8,128)S(1)}, f32[21,8,8,1]{0,2,3,1:T(8,128)S(1)}, u32[]{:S(2)}, u32[]{:S(2)}) collective-permute-start(f32[21,8,8,1]{0,2,3,1:T(8,128)S(1)} %copy.261), channel_id=1, source_target_pairs={{0,1},{1,2},{2,3},{3,0},{4,5},{5,6},{6,7},{7,4},{8,9},{9,10},{10,1... | collective-permute-start | bytes 16136 | tf_op jit(solution)/shard_map/ppermute | solution.py:17
where the time goes:
time: 57.9 us; the launch traced here: 57.4 us
  local copies, waits for them, and re-layouts  17 us (29%)
  starting transfers between devices  11 us (19%)
  other arithmetic  10.8 us (19%)
  waiting for transfers between devices  10.1 us (17%)
  blocking collectives  5.29 us (9%)
  matrix products  1.89 us (3%)
  between operations  1.01 us (2%)
    unnamed x22, local copies, waits for them, and re-layouts  8.74 us
    all_to_all x1, waiting for transfers between devices, on_device(): lax.all_to_all(packed, 'lev', split_axis=3, concat_axis=2, tiled=True)  8.13 us
    ppermute x2, starting transfers between devices, extended_2(): before = lax.ppermute(last, axis, up)  6.16 us
    all_gather x1, blocking collectives, prefix(): pieces = lax.all_gather(value, axis)  5.29 us
    all_to_all x1, starting transfers between devices, on_device(): lax.all_to_all(packed, 'lev', split_axis=3, concat_axis=2, tiled=True)  3.47 us
    all_to_all x2, local copies, waits for them, and re-layouts, on_device(): lax.all_to_all(packed, 'lev', split_axis=3, concat_axis=2, tiled=True)  2.8 us
    all_to_all x1, other arithmetic, on_device(): lax.all_to_all(packed, 'lev', split_axis=3, concat_axis=2, tiled=True)  2.16 us
    ppermute x2, waiting for transfers between devices, extended_2(): before = lax.ppermute(last, axis, up)  2.01 us
  transfers between devices with their start and end apart: 5, of which 2 were waited for; matrix products, arithmetic and copies ran while one was open for 11% of the time, Pallas kernels for 0%

commit v1 on v0

--- a/solution.py
+++ b/solution.py
@@ -87,7 +87,18 @@
     )
     density = jnp.exp(-height / scale_height)
     packed = jnp.concatenate([advected, vertical_span_height[None], density[None]], 0)
-    columns = lax.all_to_all(packed, "lev", split_axis=3, concat_axis=2, tiled=True)
+    ways, here = (lax.axis_size("lev"), lax.axis_index("lev"))
+    width_2 = packed.shape[3] // ways
+    dims = list(packed.shape)
+    dims[3] = width_2
+    height_2 = dims[2]
+    dims[2] = height_2 * ways
+    columns = jnp.zeros(dims, packed.dtype)
+    for mask in range(ways):
+        part = lax.dynamic_slice_in_dim(packed, (here ^ mask) * width_2, width_2, axis=3)
+        if mask:
+            part = lax.ppermute(part, "lev", [(d, d ^ mask) for d in range(ways)])
+        columns = lax.dynamic_update_slice_in_dim(columns, part, (here ^ mask) * height_2, axis=2)
     col_thick = columns[bin_count]
     col_density = columns[bin_count + 1]
     settle_rate = gravitational_fall_kilometres[:, None, None, None] / col_thick[None]

time: 57.9 us -> 39.2 us (0.68)
  local copies, waits for them, and re-layouts: 17 us -> 6.25 us
  other arithmetic: 10.8 us -> 2.66 us
    all_to_all x1 -> x0, waiting for transfers between devices: 8.13 us -> none  [on_device(): lax.all_to_all(packed, 'lev', split_axis=3, concat_axis=2, tiled=True)]
    ppermute x0 -> x3, waiting for transfers between devices: none -> 8.06 us  [on_device(): part = lax.ppermute(part, 'lev', [(d, d ^ mask) for d in range(ways)])]
    unnamed x22 -> x15, local copies, waits for them, and re-layouts: 8.74 us -> 3.35 us
    all_to_all x1 -> x0, starting transfers between devices: 3.47 us -> none  [on_device(): lax.all_to_all(packed, 'lev', split_axis=3, concat_axis=2, tiled=True)]
    all_to_all x2 -> x0, local copies, waits for them, and re-layouts: 2.8 us -> none  [on_device(): lax.all_to_all(packed, 'lev', split_axis=3, concat_axis=2, tiled=True)]
    ppermute x0 -> x3, starting transfers between devices: none -> 2.45 us  [on_device(): part = lax.ppermute(part, 'lev', [(d, d ^ mask) for d in range(ways)])]
    all_to_all x1 -> x0, other arithmetic: 2.16 us -> none  [on_device(): lax.all_to_all(packed, 'lev', split_axis=3, concat_axis=2, tiled=True)]
    slice x4 -> x0, local copies, waits for them, and re-layouts: 1.99 us -> none  [the longest x1 1.14 us: on_device(): settled = settle_sweep(columns[:bin_count], settle_rate, inflow)]
  transfers between devices with their start and end apart: 5 -> 7, of which waited for: 2 -> 4; matrix products, arithmetic and copies ran while one was open for 11% -> 7% of each run, Pallas kernels for 0% -> 0%
where the time goes in v1:
time: 39.2 us; the launch traced here: 38.8 us
  starting transfers between devices  10.9 us (28%)
  waiting for transfers between devices  10.5 us (27%)
  local copies, waits for them, and re-layouts  6.25 us (16%)
  blocking collectives  5.29 us (13%)
  other arithmetic  2.66 us (7%)
  matrix products  1.82 us (5%)
  between operations  1.05 us (3%)
    ppermute x3, waiting for transfers between devices, on_device(): part = lax.ppermute(part, 'lev', [(d, d ^ mask) for d in range(ways)])  8.06 us
    ppermute x2, starting transfers between devices, extended_2(): before = lax.ppermute(last, axis, up)  5.51 us
    all_gather x1, blocking collectives, prefix(): pieces = lax.all_gather(value, axis)  5.29 us
    unnamed x15, local copies, waits for them, and re-layouts  3.35 us
    ppermute x2, starting transfers between devices, extended_2(): after = lax.ppermute(leading, axis, down)  2.97 us
    ppermute x3, starting transfers between devices, on_device(): part = lax.ppermute(part, 'lev', [(d, d ^ mask) for d in range(ways)])  2.45 us
    dot_general x1, matrix products, on_device(): jnp.einsum('bc,clkx->blkx', merging, moved, precision=lax.Precision.HIGHEST)  1.82 us
    ppermute x2, waiting for transfers between devices, extended_2(): before = lax.ppermute(last, axis, up)  1.42 us
  transfers between devices with their start and end apart: 7, of which 4 were waited for; matrix products, arithmetic and copies ran while one was open for 7% of the time, Pallas kernels for 0%

profile of v1, /device:TPU:0, one launch (start us, length us, event | category | flops | bytes accessed | tf_op | source)
XLA Modules:
  0.0 38.8 jit_solution(731074193727605036)
XLA Ops:
  0.6 1.1 %copy.26 = f32[20,8,2,360]{3,1,0,2:T(8,128)S(1)} copy(f32[20,8,2,360]{3,2,1,0:T(2,128)} %param.11) | data formatting | bytes 921600 | tf_op args[0]
  1.7 0.1 pad_maximum_fusion.11
  1.8 1.3 %collective-permute-start.1 = (f32[21,1,2,360]{3,1,0,2:T(1,128)S(1)}, f32[21,1,2,360]{3,1,0,2:T(1,128)S(1)}, u32[]{:S(2)}, u32[]{:S(2)}) collective-permute-start(f32[21,1,2,360]{3,1,0,2:T(1,128)S(1)} %get-tuple-element.182), channel_id=1, source_target_pairs={{4,0},{8,4},{12,8},{16,12},{20,16},{24,20},{28,24},{5,1},{9,5},{13... | collective-permute-start | bytes 181448 | tf_op jit(solution)/shard_map/ppermute | solution.py:18
  3.1 5.5 %collective-permute-start = (f32[21,1,2,360]{3,1,0,2:T(1,128)S(1)}, f32[21,1,2,360]{3,1,0,2:T(1,128)S(1)}, u32[]{:S(2)}, u32[]{:S(2)}) collective-permute-start(f32[21,1,2,360]{3,1,0,2:T(1,128)S(1)} %get-tuple-element.181), channel_id=1, source_target_pairs={{0,4},{4,8},{8,12},{12,16},{16,20},{20,24},{24,28},{1,5},{5,9},{9,... | collective-permute-start | bytes 181448 | tf_op jit(solution)/shard_map/ppermute | solution.py:17
  8.6 0.6 %copy-done.5 = f32[2]{0:T(128)S(1)} copy-done((f32[2]{0:T(128)S(1)}, f32[2]{0:T(128)}, u32[]{:S(2)}) %copy-start.5) | copy-done | bytes 32
  9.3 0.1 fusion.31
  9.4 5.3 %all-gather = f32[32,360]{1,0:T(8,128)S(1)} all-gather(f32[8,360]{1,0:T(8,128)S(1)} %get-tuple-element.171), channel_id=2, replica_groups=mesh['lat'=8,'lev'=4] {'lev'}, dimensions={0}, use_global_device_ids=true | all-gather | bytes 57600 | tf_op jit(solution)/shard_map/all_gather | solution.py:25
  14.7 0.1 while.27
  14.8 0.2 rev.10
  15.0 0.2 rev.11
  15.2 0.6 %exponential_bitcast_fusion = (f32[1,8,2,360]{3,2,1,0:T(2,128)S(1)}, f32[8,2,360]{2,1,0:T(2,128)}) fusion(f32[8,2,360]{2,1,0:T(2,128)S(1)} %get-tuple-element.172, f32[8,2,360]{2,1,0:T(2,128)S(1)} %rev.11, f32[8,360]{1,0:T(8,128)S(1)} %get-tuple-element.108), kind=kLoop, calls=%fused_computation.49 | loop fusion | flops 28800 | bytes 103680 | tf_op jit(solution)/shard_map/broadcast_in_dim | solution.py:89
  16.0 0.3 fusion.15
  16.4 0.3 constant_dynamic-slice_fusion
  16.7 0.4 %collective-permute-start.2 = (f32[22,8,2,90]{3,1,0,2:T(8,128)S(1)}, f32[22,8,2,90]{3,1,0,2:T(8,128)S(1)}, u32[]{:S(2)}, u32[]{:S(2)}) collective-permute-start(f32[22,8,2,90]{3,1,0,2:T(8,128)S(1)} %get-tuple-element.179), channel_id=1, source_target_pairs={{0,1},{1,0},{2,3},{3,2},{4,5},{5,4},{6,7},{7,6},{8,9},{9,8},{10,11... | collective-permute-start | bytes 380168 | tf_op jit(solution)/shard_map/ppermute | solution.py:100
  17.1 2.0 %collective-permute-start.3 = (f32[22,8,2,90]{3,1,0,2:T(8,128)S(1)}, f32[22,8,2,90]{3,1,0,2:T(8,128)S(1)}, u32[]{:S(2)}, u32[]{:S(2)}) collective-permute-start(f32[22,8,2,90]{3,1,0,2:T(8,128)S(1)} %get-tuple-element.178), channel_id=1, source_target_pairs={{0,2},{1,3},{2,0},{3,1},{4,6},{5,7},{6,4},{7,5},{8,10},{9,11},{10,... | collective-permute-start | bytes 380168 | tf_op jit(solution)/shard_map/ppermute | solution.py:100
  19.3 5.2 %collective-permute-done.3 = f32[22,8,2,90]{3,1,0,2:T(8,128)S(1)} collective-permute-done((f32[22,8,2,90]{3,1,0,2:T(8,128)S(1)}, f32[22,8,2,90]{3,1,0,2:T(8,128)S(1)}, u32[]{:S(2)}, u32[]{:S(2)}) %collective-permute-start.3) | collective-permute-done | bytes 126752 | tf_op jit(solution)/shard_map/ppermute | solution.py:100
  24.5 2.9 %collective-permute-done.4 = f32[22,8,2,90]{3,1,0,2:T(8,128)S(1)} collective-permute-done((f32[22,8,2,90]{3,1,0,2:T(8,128)S(1)}, f32[22,8,2,90]{3,1,0,2:T(8,128)S(1)}, u32[]{:S(2)}, u32[]{:S(2)}) %collective-permute-start.4) | collective-permute-done | bytes 126752 | tf_op jit(solution)/shard_map/ppermute | solution.py:100
  27.5 0.6 %copy-done.3 = f32[20]{0:T(128)S(1)} copy-done((f32[20]{0:T(128)S(1)}, f32[20]{0:T(128)}, u32[]{:S(2)}) %copy-start.3) | copy-done | bytes 104
  28.1 0.1 broadcast_divide_fusion
  28.2 0.8 %while.28 = (s32[]{:T(128)}, f32[20,8,90]{2,1,0:T(8,128)S(1)}, f32[8,20,8,90]{3,2,1,0:T(8,128)S(1)}, f32[8,20,8,90]{3,2,1,0:T(8,128)S(1)}, f32[8,20,8,90]{3,2,1,0:T(8,128)S(1)}, /*index=5*/s32[]{:T(128)}, s32[]{:T(128)}) while((s32[]{:T(128)}, f32[20,8,90]{2,1,0:T(8,128)S(1)}, f32[8,20,8,90]{3,2,1,0:T(8,128)S(1)}, ...), condition=%wide.region_5.6_spmd.clone, body=%wide.region_4.5_spmd.clone.sunk | while | flops 129603 | bytes 558176 | solution.py:44
  29.0 0.1 copy.40
  29.2 0.4 slice_maximum_fusion
  29.5 0.5 %copy.33 = f32[21,8,8,1]{0,2,3,1:T(8,128)S(1)} copy(f32[21,8,8,1]{3,0,2,1:T(8,128)S(1)} %get-tuple-element.174) | data formatting | bytes 10752 | tf_op jit(solution)/shard_map/slice | solution.py:16
  30.0 1.7 %collective-permute-start.6 = (f32[21,8,8,1]{0,2,3,1:T(8,128)S(1)}, f32[21,8,8,1]{0,2,3,1:T(8,128)S(1)}, u32[]{:S(2)}, u32[]{:S(2)}) collective-permute-start(f32[21,8,8,1]{0,2,3,1:T(8,128)S(1)} %copy.33), channel_id=1, source_target_pairs={{1,0},{2,1},{3,2},{0,3},{5,4},{6,5},{7,6},{4,7},{9,8},{10,9},{11,1... | collective-permute-start | bytes 16136 | tf_op jit(solution)/shard_map/ppermute | solution.py:18
  31.7 0.5 %copy.31 = f32[21,8,8,1]{0,2,3,1:T(8,128)S(1)} copy(f32[21,8,8,1]{3,0,2,1:T(8,128)S(1)} %get-tuple-element.173) | data formatting | bytes 10752 | tf_op jit(solution)/shard_map/slice | solution.py:15
  32.2 1.1 %collective-permute-done.6 = f32[21,8,8,1]{0,2,3,1:T(8,128)S(1)} collective-permute-done((f32[21,8,8,1]{0,2,3,1:T(8,128)S(1)}, f32[21,8,8,1]{0,2,3,1:T(8,128)S(1)}, u32[]{:S(2)}, u32[]{:S(2)}) %collective-permute-start.6) | collective-permute-done | bytes 5408 | tf_op jit(solution)/shard_map/ppermute | solution.py:18
  33.3 0.5 %copy.34 = f32[21,8,8,1]{3,0,2,1:T(8,128)S(1)} copy(f32[21,8,8,1]{0,2,3,1:T(8,128)S(1)} %collective-permute-done.6) | data formatting | bytes 10752 | tf_op jit(solution)/shard_map/ppermute | solution.py:18
  33.8 0.3 broadcast_maximum_fusion
  34.1 1.4 %collective-permute-done.5 = f32[21,8,8,1]{0,2,3,1:T(8,128)S(1)} collective-permute-done((f32[21,8,8,1]{0,2,3,1:T(8,128)S(1)}, f32[21,8,8,1]{0,2,3,1:T(8,128)S(1)}, u32[]{:S(2)}, u32[]{:S(2)}) %collective-permute-start.5) | collective-permute-done | bytes 5408 | tf_op jit(solution)/shard_map/ppermute | solution.py:17
  35.6 0.5 %copy.32 = f32[21,8,8,1]{3,0,2,1:T(8,128)S(1)} copy(f32[21,8,8,1]{0,2,3,1:T(8,128)S(1)} %collective-permute-done.5) | data formatting | bytes 10752 | tf_op jit(solution)/shard_map/ppermute | solution.py:17
  36.1 1.8 %fusion.3 = f32[20,8,8,90]{3,0,2,1:T(8,128)S(1)} fusion(f32[21,8,8,1]{3,0,2,1:T(8,128)S(1)} %copy.34, f32[1,8,8,90]{3,0,2,1:T(1,128)S(1)} %bitcast.66, f32[20,8,8,90]{3,0,2,1:T(8,128)S(1)} %bitcast.59, f32[21,8,8,1]{3,0,2,1:T(8,128)S(1)} %copy.32, f32[8,8,90]{2,1,0:T(8,128)S(1)} %copy.35, f32[8,8,90]{2,1,0:T(8,128)S(1)} %bitcast.69, ...), kind=kOutput, calls=%fused_computation.8 | convolution fusion | flops 30760400 | bytes 1072272 | tf_op jit(solution)/shard_map/bc,clkx->blkx/dot_general | solution.py:119
  37.9 1.0 %copy.36 = f32[20,8,8,90]{3,2,1,0:T(8,128)} copy(f32[20,8,8,90]{3,0,2,1:T(8,128)S(1)} %fusion.3) | data formatting | bytes 921600
  (59 shorter events, 1.1 us)
Async XLA Ops:
  0.6 1.1 %copy-start.1 = (f32[8,2,360]{2,1,0:T(2,128)S(1)}, f32[8,2,360]{2,1,0:T(2,128)}, u32[]{:S(2)}) copy-start(f32[8,2,360]{2,1,0:T(2,128)} %param.12) | copy-start | bytes 69124
  1.7 7.6 %copy-start.2 = (f32[8,2,360]{2,1,0:T(2,128)S(1)}, f32[8,2,360]{2,1,0:T(2,128)}, u32[]{:S(2)}) copy-start(f32[8,2,360]{2,1,0:T(2,128)} %param.13) | copy-start | bytes 69124
  1.8 14.1 %collective-permute-start.1 = (f32[21,1,2,360]{3,1,0,2:T(1,128)S(1)}, f32[21,1,2,360]{3,1,0,2:T(1,128)S(1)}, u32[]{:S(2)}, u32[]{:S(2)}) collective-permute-start(f32[21,1,2,360]{3,1,0,2:T(1,128)S(1)} %get-tuple-element.182), channel_id=1, source_target_pairs={{4,0},{8,4},{12,8},{16,12},{20,16},{24,20},{28,24},{5,1},{9,5},{13... | collective-permute-start | bytes 181448 | tf_op jit(solution)/shard_map/ppermute | solution.py:18
  3.1 12.9 %collective-permute-start = (f32[21,1,2,360]{3,1,0,2:T(1,128)S(1)}, f32[21,1,2,360]{3,1,0,2:T(1,128)S(1)}, u32[]{:S(2)}, u32[]{:S(2)}) collective-permute-start(f32[21,1,2,360]{3,1,0,2:T(1,128)S(1)} %get-tuple-element.181), channel_id=1, source_target_pairs={{0,4},{4,8},{8,12},{12,16},{16,20},{20,24},{24,28},{1,5},{5,9},{9,... | collective-permute-start | bytes 181448 | tf_op jit(solution)/shard_map/ppermute | solution.py:17
  8.6 0.7 %copy-start.5 = (f32[2]{0:T(128)S(1)}, f32[2]{0:T(128)}, u32[]{:S(2)}) copy-start(f32[2]{0:T(128)} %param.14) | copy-start | bytes 28
  16.4 2.7 %copy-start = (f32[8,8,90]{2,1,0:T(8,128)S(1)}, f32[8,8,90]{2,1,0:T(8,128)}, u32[]{:S(2)}) copy-start(f32[8,8,90]{2,1,0:T(8,128)} %param.16) | copy-start | bytes 69124
  16.7 2.5 %collective-permute-start.2 = (f32[22,8,2,90]{3,1,0,2:T(8,128)S(1)}, f32[22,8,2,90]{3,1,0,2:T(8,128)S(1)}, u32[]{:S(2)}, u32[]{:S(2)}) collective-permute-start(f32[22,8,2,90]{3,1,0,2:T(8,128)S(1)} %get-tuple-element.179), channel_id=1, source_target_pairs={{0,1},{1,0},{2,3},{3,2},{4,5},{5,4},{6,7},{7,6},{8,9},{9,8},{10,11... | collective-permute-start | bytes 380168 | tf_op jit(solution)/shard_map/ppermute | solution.py:100
  17.1 7.4 %collective-permute-start.3 = (f32[22,8,2,90]{3,1,0,2:T(8,128)S(1)}, f32[22,8,2,90]{3,1,0,2:T(8,128)S(1)}, u32[]{:S(2)}, u32[]{:S(2)}) collective-permute-start(f32[22,8,2,90]{3,1,0,2:T(8,128)S(1)} %get-tuple-element.178), channel_id=1, source_target_pairs={{0,2},{1,3},{2,0},{3,1},{4,6},{5,7},{6,4},{7,5},{8,10},{9,11},{10,... | collective-permute-start | bytes 380168 | tf_op jit(solution)/shard_map/ppermute | solution.py:100
  19.2 8.2 %collective-permute-start.4 = (f32[22,8,2,90]{3,1,0,2:T(8,128)S(1)}, f32[22,8,2,90]{3,1,0,2:T(8,128)S(1)}, u32[]{:S(2)}, u32[]{:S(2)}) collective-permute-start(f32[22,8,2,90]{3,1,0,2:T(8,128)S(1)} %get-tuple-element.177), channel_id=1, source_target_pairs={{0,3},{1,2},{2,1},{3,0},{4,7},{5,6},{6,5},{7,4},{8,11},{9,10},{10,... | collective-permute-start | bytes 380168 | tf_op jit(solution)/shard_map/ppermute | solution.py:100
  27.5 0.7 %copy-start.3 = (f32[20]{0:T(128)S(1)}, f32[20]{0:T(128)}, u32[]{:S(2)}) copy-start(f32[20]{0:T(128)} %param.15) | copy-start | bytes 244
  30.0 3.3 %collective-permute-start.6 = (f32[21,8,8,1]{0,2,3,1:T(8,128)S(1)}, f32[21,8,8,1]{0,2,3,1:T(8,128)S(1)}, u32[]{:S(2)}, u32[]{:S(2)}) collective-permute-start(f32[21,8,8,1]{0,2,3,1:T(8,128)S(1)} %copy.33), channel_id=1, source_target_pairs={{1,0},{2,1},{3,2},{0,3},{5,4},{6,5},{7,6},{4,7},{9,8},{10,9},{11,1... | collective-permute-start | bytes 16136 | tf_op jit(solution)/shard_map/ppermute | solution.py:18
  32.2 3.4 %collective-permute-start.5 = (f32[21,8,8,1]{0,2,3,1:T(8,128)S(1)}, f32[21,8,8,1]{0,2,3,1:T(8,128)S(1)}, u32[]{:S(2)}, u32[]{:S(2)}) collective-permute-start(f32[21,8,8,1]{0,2,3,1:T(8,128)S(1)} %copy.31), channel_id=1, source_target_pairs={{0,1},{1,2},{2,3},{3,0},{4,5},{5,6},{6,7},{7,4},{8,9},{9,10},{10,1... | collective-permute-start | bytes 16136 | tf_op jit(solution)/shard_map/ppermute | solution.py:17
  34.1 1.9 %copy-start.4 = (f32[20,20]{1,0:T(8,128)S(1)}, f32[20,20]{1,0:T(8,128)}, u32[]{:S(2)}) copy-start(f32[20,20]{1,0:T(8,128)} %param.17) | copy-start | bytes 4804
